TPU v7x, 32 devices: a whole 2x2x4 slice. The times are simulated.
32 devices in a mesh: row: 4 (over y, x), col: 8 (over z, core).
Axes of the slice: x: 2, y: 2, z: 4, core: 2. Of those that a mesh axis runs over, the one named last changes fastest.
Arguments:
- ancestor: float32 [20480, 20480], P('row', 'col'), as said below
- factor_rows: float32 [2, 256, 20480], P(None, 'row', 'col'), may hold values from -6 to 6
- block_lists: int32 [2, 8], replicated, may hold values from 0 to 15, as said below
Outputs:
- inverse_panel: float32 [2, 20480, 256], P(None, ('row', 'col'))
- inverse_rows: float32 [2, 256, 20480], P(None, 'col', 'row')
Inputs may be any that keep to these rules, and one draw needn't show every extreme that they name: `block_lists`: each row lists 8 distinct blocks in increasing order; the first block 0 and the last block 15 are in every row. ancestor is symmetric: ancestor[i, j] = ancestor[j, i].
All inputs are finite; a program needn't handle non-finite values.
Results may differ from a plain program's by a relative error of at most 0.000071.
Values sent between devices are 32-bit elements; how exact they have to be, the bound alone decides.
No kernel may reach another device: no remote copies, remote signals or barrier semaphores. Data moves between devices by JAX's collectives and lax.ppermute only.
A program may use at most 128 MiB of HBM per device.

v0:
```python
import functools

import jax
import jax.numpy as jnp
from jax import lax
from jax.experimental import pallas as pl
from jax.experimental.pallas import tpu as pltpu
from jax.sharding import PartitionSpec as P

BS = 1280
F32 = jnp.float32
BF16 = jnp.bfloat16
I32 = jnp.int32
VMEM_LIMIT = 20 * 1024 * 1024
PARAMS = pltpu.CompilerParams(vmem_limit_bytes=VMEM_LIMIT)
LAGS = (2, 3, 5)
PRODUCT_FLOPS = 0
RELAY_AT = 2
ANY = pl.BlockSpec(memory_space=pl.ANY)


def tile_of(extent, wanted, step):
    best = extent
    for size in range(step, wanted + 1, step):
        if extent % size == 0:
            best = size
    return best


def cost(bytes_accessed):
    return pl.CostEstimate(flops=0, bytes_accessed=bytes_accessed, transcendentals=0)


def copy_kernel(source, target):
    target[...] = source[0]


def share_of(factor_rows, member):
    share, cols = factor_rows.shape[1:]
    return pl.pallas_call(
        copy_kernel,
        grid=(1,),
        in_specs=[pl.BlockSpec((1, share, cols), lambda i: (member, 0, 0))],
        out_specs=pl.BlockSpec((share, cols), lambda i: (0, 0)),
        out_shape=jax.ShapeDtypeStruct((share, cols), F32),
        compiler_params=PARAMS,
        cost_estimate=cost(1024),
        name="own_share",
    )(factor_rows)


def prep_kernel(places, share, following, base, units, bits, meta_ref, *refs):
    pieces = refs[: len(places)]
    rest = refs[len(places) :]
    if following:
        next_in, high_ref, low_ref, next_out, whole = rest
        next_out[...] = next_in[0]
    else:
        high_ref, low_ref, whole = rest
    me = meta_ref[base + 2]
    row = meta_ref[base + 3]
    step = pl.program_id(0)
    rows = whole.shape[0] >> bits
    for (mask, offset), piece in zip(places, pieces):
        first = (row ^ mask) * share + offset
        for at in range(0, piece.shape[0], rows):
            flip = ((first + at) // rows) ^ me
            turned_flip = sum(((flip >> bit) & 1) << (bits - 1 - bit) for bit in range(bits))
            whole[pl.ds(pl.multiple_of(turned_flip * rows, rows), rows), :] = piece[at : at + rows, :]
    scale = jnp.where(meta_ref[base + 4 + step] > 0, -1.0, 0.0).astype(F32)
    turned = whole[...].T * scale
    high = turned.astype(BF16)
    high_ref[...] = high
    low_ref[...] = (turned - high.astype(F32)).astype(BF16)


def prepare(base, meta, factor_rows, own, received, width, unit, bits, following):
    share, cols = own.shape
    units = cols // unit
    places = [(0, 0)] + [(mask, offset) for mask, offset, _ in received]
    arrays = [own] + [piece for _, _, piece in received]
    in_specs = [pl.BlockSpec((piece.shape[0], unit), lambda i, m: (0, i)) for piece in arrays]
    out_specs = [pl.BlockSpec((unit, width), lambda i, m: (i, 0))] * 2
    out_shape = [jax.ShapeDtypeStruct((cols, width), BF16)] * 2
    if following is not None:
        arrays.append(factor_rows)
        in_specs.append(pl.BlockSpec((1, share, unit), lambda i, m: (following, 0, i)))
        out_specs.append(pl.BlockSpec((share, unit), lambda i, m: (0, i)))
        out_shape.append(jax.ShapeDtypeStruct((share, cols), F32))
    outs = pl.pallas_call(
        functools.partial(prep_kernel, places, share, following is not None, base, units, bits),
        grid_spec=pltpu.PrefetchScalarGridSpec(
            num_scalar_prefetch=1,
            grid=(units,),
            in_specs=in_specs,
            out_specs=out_specs,
            scratch_shapes=[pltpu.VMEM((width, unit), F32)],
        ),
        out_shape=out_shape,
        compiler_params=PARAMS,
        cost_estimate=cost(1024),
        name="prepare_factor",
    )(meta, *arrays)
    return outs if following is not None else (*outs, None)


def slot_kernel(base, tile, deps, meta_ref, a_ref, high_ref, low_ref, *refs):
    mine_ref, theirs_ref, buffer, total, arrived = refs[deps:]
    half, rows, block = mine_ref.shape
    tiles = block // tile
    depth = buffer.shape[0]
    first = meta_ref[base] * block

    def copy(t):
        source = a_ref.at[pl.ds(pl.multiple_of(first + t * tile, tile), tile), :]
        slot = lax.rem(t, depth)
        return pltpu.make_async_copy(source, buffer.at[slot], arrived.at[slot])

    def turn(t):
        turned = total[lax.rem(t, 2)].T
        columns = pl.ds(pl.multiple_of(t * tile, tile), tile)
        mine_ref[:, :, columns] = turned[: half * rows].reshape(half, rows, tile)
        theirs_ref[:, :, columns] = turned[half * rows :].reshape(half, rows, tile)

    def product(t):
        a = buffer[lax.rem(t, depth)]
        a_high = a.astype(BF16)
        a_low = (a - a_high.astype(F32)).astype(BF16)
        dot = functools.partial(jnp.dot, preferred_element_type=F32)
        total[lax.rem(t, 2)] = (
            dot(a_high, high_ref[...]) + dot(a_high, low_ref[...]) + dot(a_low, high_ref[...])
        )

    valid = meta_ref[base + 1] > 0

    @pl.when(valid)
    def _():
        for t in range(min(depth - 1, tiles)):
            copy(t).start()

        def step(t, carry):
            @pl.when(t + depth - 1 < tiles)
            def _():
                copy(t + depth - 1).start()

            copy(t).wait()
            product(t)
            turn(lax.max(t - 1, 0))
            return carry

        lax.fori_loop(0, tiles, step, 0)
        turn(tiles - 1)

    @pl.when(jnp.logical_not(valid))
    def _():
        mine_ref[...] = jnp.zeros_like(mine_ref)
        theirs_ref[...] = jnp.zeros_like(theirs_ref)


def slot_product(base, meta, ancestor, high, low, chunks, block, after):
    cols, width = high.shape
    tile = tile_of(block, 256, 128)
    rows = width // chunks
    half = chunks // 2
    in_vmem = pl.BlockSpec(memory_space=pltpu.VMEM)
    return pl.pallas_call(
        functools.partial(slot_kernel, base, tile, len(after)),
        grid_spec=pltpu.PrefetchScalarGridSpec(
            num_scalar_prefetch=1,
            grid=(1,),
            in_specs=[ANY, in_vmem, in_vmem] + [ANY] * len(after),
            out_specs=[in_vmem, in_vmem],
            scratch_shapes=[
                pltpu.VMEM((3, tile, cols), F32),
                pltpu.VMEM((2, tile, width), F32),
                pltpu.SemaphoreType.DMA((3,)),
            ],
        ),
        out_shape=[jax.ShapeDtypeStruct((half, rows, block), F32)] * 2,
        compiler_params=PARAMS,
        cost_estimate=pl.CostEstimate(
            flops=PRODUCT_FLOPS, bytes_accessed=4 * block * cols, transcendentals=0
        ),
        name="slot_product",
    )(meta, ancestor, high, low, *after)


def place_kernel(base, fields, terms, ignored, meta_ref, *refs):
    count = len(terms)
    parts = [refs[sum(terms[:k]) : sum(terms[: k + 1])] for k in range(count)]
    outs = refs[sum(terms) + ignored :]
    rows_ref, sends = outs[0], outs[1:]
    groups = rows_ref.shape[2] // parts[0][0].shape[2]
    block = parts[0][0].shape[2]
    place = meta_ref[base + 2] // 2
    rows_ref[...] = jnp.zeros_like(rows_ref)
    for send in sends:
        send[...] = jnp.zeros_like(send)
    for k in range(count):
        at = meta_ref[base + k * fields]

        @pl.when(meta_ref[base + k * fields + 1] > 0)
        def _(k=k, at=at):
            total = parts[k][0][0]
            for term in parts[k][1:]:
                total = total + term[0]
            for g in range(groups):

                @pl.when(at == g)
                def _():
                    rows_ref[0, :, g * block : (g + 1) * block] = total

            for flip, send in enumerate(sends):

                @pl.when(at == (place ^ flip))
                def _():
                    send[...] = total


def place_slots(base, fields, meta, parts, member, members, previous, local_rows, line, exchange, after):
    rows, block = parts[0][0].shape[1:]
    terms = [len(part) for part in parts]
    arrays = [term for part in parts for term in part]
    first = pl.BlockSpec((1, rows, block), lambda i, meta_ref: (0, 0, 0))
    in_specs = [first] * len(arrays)
    aliases = {}
    if previous is not None:
        aliases = {1 + len(arrays): 0}
        arrays.append(previous)
        in_specs.append(ANY)
    arrays += after
    in_specs += [ANY] * len(after)
    ignored = len(after) + (previous is not None)
    out_specs = [pl.BlockSpec((1, rows, local_rows), lambda i, meta_ref: (member, 0, 0))]
    out_shape = [jax.ShapeDtypeStruct((members, rows, local_rows), F32)]
    if exchange:
        out_specs += [pl.BlockSpec((rows, block), lambda i, meta_ref: (0, 0))] * line
        out_shape += [jax.ShapeDtypeStruct((rows, block), F32)] * line
    return pl.pallas_call(
        functools.partial(place_kernel, base, fields, terms, ignored),
        grid_spec=pltpu.PrefetchScalarGridSpec(
            num_scalar_prefetch=1, grid=(1,), in_specs=in_specs, out_specs=out_specs
        ),
        out_shape=out_shape,
        input_output_aliases=aliases,
        compiler_params=PARAMS,
        cost_estimate=cost(1024),
        name="place_slots",
    )(meta, *arrays)


def split_kernel(core_ref, *refs):
    pieces, out = refs[:-1], refs[-1]
    half = out.shape[2]
    for at, piece in enumerate(pieces):
        for core in range(2):

            @pl.when(core_ref[0] == core)
            def _():
                out[at] = piece[:, (1 - core) * half : (2 - core) * half]


def split_halves(core, pieces):
    rows, block = pieces[0].shape
    whole = pl.BlockSpec((rows, block), lambda i, core_ref: (0, 0))
    shape = (len(pieces), rows, block // 2)
    return pl.pallas_call(
        split_kernel,
        grid_spec=pltpu.PrefetchScalarGridSpec(
            num_scalar_prefetch=1,
            grid=(1,),
            in_specs=[whole] * len(pieces),
            out_specs=pl.BlockSpec(shape, lambda i, core_ref: (0, 0, 0)),
        ),
        out_shape=jax.ShapeDtypeStruct(shape, F32),
        compiler_params=PARAMS,
        cost_estimate=cost(1024),
        name="split_halves",
    )(core.reshape(1), *pieces)


def panel_kernel(line, col_ref, *refs):
    pieces, swapped, out, whole = refs[:line], refs[line], refs[-2], refs[-1]
    rows = pieces[0].shape[0]
    half = swapped.shape[2]
    me = col_ref[0]
    core = me % 2
    for flip, piece in enumerate(pieces):
        for side in range(2):

            @pl.when(core == side)
            def _():
                first = pl.multiple_of((me ^ (2 * flip)) * rows, rows)
                whole[pl.ds(first, rows), :] = piece[:, side * half : (side + 1) * half]

        first = pl.multiple_of((me ^ (2 * flip + 1)) * rows, rows)
        whole[pl.ds(first, rows), :] = swapped[flip]
    out[0] = whole[...].T


def place_panel(col_place, pieces, swapped, member, members, previous):
    line = len(pieces)
    rows, block = pieces[0].shape
    half = block // 2
    width = 2 * line * rows
    arrays = list(pieces) + [swapped]
    in_specs = [pl.BlockSpec((rows, block), lambda i, col_ref: (0, 0))] * line
    in_specs.append(pl.BlockSpec(swapped.shape, lambda i, col_ref: (0, 0, 0)))
    aliases = {}
    if previous is not None:
        aliases = {1 + len(arrays): 0}
        arrays.append(previous)
        in_specs.append(ANY)
    return pl.pallas_call(
        functools.partial(panel_kernel, line),
        grid_spec=pltpu.PrefetchScalarGridSpec(
            num_scalar_prefetch=1,
            grid=(1,),
            in_specs=in_specs,
            out_specs=pl.BlockSpec((1, half, width), lambda i, col_ref: (member, 0, 0)),
            scratch_shapes=[pltpu.VMEM((width, half), F32)],
        ),
        out_shape=jax.ShapeDtypeStruct((members, half, width), F32),
        input_output_aliases=aliases,
        compiler_params=PARAMS,
        cost_estimate=cost(1024),
        name="place_panel",
    )(col_place.reshape(1), *arrays)


def halves_kernel(deps, first, second, *refs):
    first_out, second_out = refs[deps:]
    first_out[...] = first[...]
    second_out[...] = second[...]


def gather_rows(mine, count, after):
    half, cols = mine.shape[0] // 2, mine.shape[1]
    pieces = {}
    received, relayed = [], []

    def swap(value, mask):
        return lax.ppermute(value, "row", [(i, i ^ mask) for i in range(count)])

    for mask in sorted(range(1, count), key=lambda m: m.bit_count()):
        if mask.bit_count() == 1:
            whole = swap(mine, mask)
            pieces[mask] = ((whole, 0), (whole, 1))
            received.append((mask, 0, whole))
        else:
            least = mask & -mask
            most = 1 << (mask.bit_length() - 1)
            first, first_at = pieces[mask ^ most][0]
            second, second_at = pieces[mask ^ least][1]
            out = pl.BlockSpec((half, cols), lambda i: (0, 0))
            first, second = pl.pallas_call(
                functools.partial(halves_kernel, len(after)),
                grid=(1,),
                in_specs=[
                    pl.BlockSpec((half, cols), lambda i, at=first_at: (at, 0)),
                    pl.BlockSpec((half, cols), lambda i, at=second_at: (at, 0)),
                ]
                + [ANY] * len(after),
                out_specs=[out, out],
                out_shape=[jax.ShapeDtypeStruct((half, cols), F32)] * 2,
                compiler_params=PARAMS,
                cost_estimate=cost(1024),
                name="relay_halves",
            )(first, second, *after)
            relayed += [first, second]
            first, second = swap(first, most), swap(second, least)
            pieces[mask] = ((first, 0), (second, 0))
            received.append((mask, 0, first))
            received.append((mask, half, second))
    return received, relayed


def swap_col(value, flip, count):
    return lax.ppermute(value, "col", [(c, c ^ flip) for c in range(count)])


def halved_sum(mine, theirs, count):
    arrived = [swap_col(theirs, 1, count)]
    terms = [mine, arrived[0]]
    flip = 2
    while flip < count:
        half = terms[-1].shape[0] // 2
        payload = sum(term[half : 2 * half] for term in terms)
        arrived.append(swap_col(payload, flip, count))
        terms.append(arrived[-1])
        flip *= 2
    return arrived, [sum(term[:1] for term in terms[:-1]), terms[-1][:1]]


def listed_in(block_lists, blocks):
    return jnp.any(block_lists[:, :, None] == blocks[None, None, :], axis=1)


def per_device(ancestor, factor_rows, block_lists):
    members, share, local_cols = factor_rows.shape
    local_rows = ancestor.shape[0]
    row_count, col_count = lax.axis_size("row"), lax.axis_size("col")
    row_place, col_place = lax.axis_index("row"), lax.axis_index("col")
    width = share * row_count
    line = col_count // 2
    core = col_place % 2
    block = min(BS, local_rows)
    groups = local_rows // block
    unit = min(BS, local_cols)
    units = local_cols // unit
    rows_out = local_rows // col_count
    exchange = 2 * rows_out == block
    bits = col_count.bit_length() - 1

    row_blocks = (row_place * local_rows + block * lax.iota(I32, groups)) // BS
    col_blocks = (col_place * local_cols + unit * lax.iota(I32, units)) // BS
    row_listed = listed_in(block_lists, row_blocks)
    col_listed = listed_in(block_lists, col_blocks).astype(I32)
    rank = jnp.cumsum(row_listed.astype(I32), axis=1) - 1
    slots = lax.iota(I32, groups)
    chosen = row_listed[:, None, :] & (rank[:, None, :] == slots[None, :, None])
    slot_block = jnp.sum(chosen * slots[None, None, :], axis=2)
    slot_valid = jnp.any(chosen, axis=2)
    fields = 4 + units
    meta = jnp.concatenate(
        [
            slot_block[:, :, None],
            slot_valid[:, :, None].astype(I32),
            jnp.broadcast_to(col_place, (members, groups, 1)).astype(I32),
            jnp.broadcast_to(row_place, (members, groups, 1)).astype(I32),
            jnp.broadcast_to(col_listed[:, None, :], (members, groups, units)),
        ],
        axis=2,
    ).reshape(-1)

    usual = groups if groups <= 1 else groups - 1
    group_of = block_lists * BS // local_rows
    held = jnp.sum(group_of[:, :, None] == lax.iota(I32, row_count)[None, None, :], axis=1)
    fullest = jnp.max(held, axis=1)
    out_rows = width // col_count

    def slot_sum(s, k, factors, after):
        base = (s * groups + k) * fields
        mine, theirs = slot_product(base, meta, ancestor, *factors, col_count, block, after)
        return halved_sum(mine, theirs, col_count)

    def rest(s, factors):
        def taken():
            return [sum(slot_sum(s, k, factors, [])[1]) for k in range(usual, groups)]

        def left():
            return [jnp.zeros((1, out_rows, block), F32) for _ in range(usual, groups)]

        if usual == groups:
            return []
        return [[total] for total in lax.cond(fullest[s] > usual, taken, left)]

    def exchange_of(placed):
        pieces = [placed[1]]
        for flip in range(1, line):
            pieces.append(swap_col(placed[1 + flip], 2 * flip, col_count))
        return pieces

    done, parts, others, placed, pieces = [], [], [], [], []

    def place(s):
        placed.append(
            place_slots(
                s * groups * fields,
                fields,
                meta,
                parts[s] + others[s],
                s,
                members,
                placed[s - 1][0] if s > 0 else None,
                local_rows,
                line,
                exchange,
                [],
            )
        )
        if exchange:
            pieces.append(exchange_of(placed[s]))

    own = share_of(factor_rows, 0)
    received, relayed = gather_rows(own, row_count, [])
    for s in range(members):
        following = s + 1 if s + 1 < members else None
        high, low, own = prepare(
            s * groups * fields, meta, factor_rows, own, received, width, unit, bits, following
        )
        parts.append([])
        for k in range(usual):
            after = []
            for step, lag in enumerate(LAGS):
                if 0 < lag <= len(done) and step < len(done[-lag]):
                    after.append(done[-lag][step])
            if following is not None and k == min(RELAY_AT, usual - 1):
                received, relayed = gather_rows(own, row_count, [])
                after += relayed[:1]
            if s > 0 and k == usual - 1:
                place(s - 1)
            arrived, terms = slot_sum(s, k, (high, low), after)
            done.append(arrived)
            parts[s].append(terms)
            if k == 0:
                others.append(rest(s, (high, low)))
    place(members - 1)
    rows_all = placed[-1][0]

    panel = None
    panel_parts = []
    for s in range(members):
        if exchange:
            swapped = swap_col(split_halves(core, pieces[s]), 1, col_count)
            panel = place_panel(col_place, pieces[s], swapped, s, members, panel)
        else:
            outgoing = rows_all[s].reshape(out_rows, col_count, rows_out)
            arrived = lax.all_to_all(outgoing, "col", split_axis=1, concat_axis=0, tiled=True)
            panel_parts.append(arrived.reshape(width, rows_out).T)
    if not exchange:
        panel = jnp.stack(panel_parts)
    return panel, rows_all


def solution(mesh):
    in_specs = (P("row", "col"), P(None, "row", "col"), P())
    out_specs = (P(None, ("row", "col"), None), P(None, "col", "row"))
    return jax.shard_map(
        per_device, mesh=mesh, in_specs=in_specs, out_specs=out_specs, check_vma=False
    )
```

profile of v0, /device:TPU:0, one launch (start us, length us, event | category | flops | bytes accessed | tf_op | source)
XLA Modules:
  0.0 173.1 jit_solution(9993511227233240844)
XLA Ops:
  0.6 1.3 copy-done
  2.0 3.0 %collective-permute-start.7 = (f32[64,2560]{1,0:T(8,128)S(1)}, f32[64,2560]{1,0:T(8,128)S(1)}, u32[]{:S(2)}, u32[]{:S(2)}) collective-permute-start(f32[64,2560]{1,0:T(8,128)S(1)} %own_share.1.refs_0_), channel_id=1, source_target_pairs={{0,16},{8,24},{16,0},{24,8},{1,17},{9,25},{17,1},{25,9},{2,18},{10... | collective-permute-start | bytes 1966088 | tf_op jit(solution)/shard_map/ppermute | solution.py:343
  5.0 1.5 collective-permute-start.6
  6.5 0.2 compare_reduce_fusion
  6.8 0.2 compare_reduce_fusion.1
  7.0 0.2 reduce_window_sum.11
  7.1 0.1 fusion.3
  7.3 12.5 %collective-permute-done.7.second.refs_2_ = f32[64,2560]{1,0:T(8,128)S(1)} collective-permute-done((f32[64,2560]{1,0:T(8,128)S(1)}, f32[64,2560]{1,0:T(8,128)S(1)}, u32[]{:S(2)}, u32[]{:S(2)}) %collective-permute-start.7) | collective-permute-done | bytes 655392 | tf_op jit(solution)/shard_map/ppermute | solution.py:343
  19.8 1.5 collective-permute-done.6.first.refs_1_
  21.2 0.9 relay_halves.2
  22.1 0.4 collective-permute-start.8
  22.5 1.6 collective-permute-start.9
  24.1 0.1 copy.10
  24.2 0.1 select_reduce_fusion
  24.3 0.1 copy.9
  24.5 0.1 concatenate.3
  24.6 6.0 %collective-permute-done.8.refs_3_ = f32[32,2560]{1,0:T(8,128)} collective-permute-done((f32[32,2560]{1,0:T(8,128)}, f32[32,2560]{1,0:T(8,128)}, u32[]{:S(2)}, u32[]{:S(2)}) %collective-permute-start.8) | collective-permute-done | bytes 327712 | tf_op jit(solution)/shard_map/ppermute | solution.py:343
  30.7 0.4 collective-permute-done.9.refs_4_
  31.1 3.5 %prepare_factor.2 = (bf16[2560,256]{1,0:T(8,128)(2,1)S(1)}, bf16[2560,256]{1,0:T(8,128)(2,1)S(1)}, f32[64,2560]{1,0:T(8,128)}) custom-call(s32[48]{0:T(128)S(1)} %reshape.75.meta_ref, f32[64,2560]{1,0:T(8,128)S(1)} %own_share.1.refs_0_, f32[64,2560]{1,0:T(8,128)S(1)} %collective-permute-done.6.first.refs_1_, ...), custom_call_target="tpu_custom_call" | custom-call | bytes 1024 | tf_op jit(solution)/shard_map/prepare_factor/pallas_call | solution.py:90
  34.6 1.3 collective-permute-start.11
  35.9 1.5 collective-permute-start.10
  37.4 9.9 %slot_product.11 = (f32[4,32,1280]{2,1,0:T(8,128)S(1)}, f32[4,32,1280]{2,1,0:T(8,128)}) custom-call(s32[48]{0:T(128)S(1)} %reshape.75.meta_ref, f32[5120,2560]{1,0:T(8,128)} %a_ref.11, bf16[2560,256]{1,0:T(8,128)(2,1)S(1)} %get-tuple-element.74.high_ref, bf16[2560,256]{1,0:T(8,128)(2,1)S(1)} %get-tuple-element.75.low_ref), custom_call_target="tpu_custom_call" | custom-call | bytes 13107200 | tf_op jit(solution)/shard_map/slot_product/pallas_call | solution.py:166
  47.4 1.5 slot_product.10
  48.9 0.6 collective-permute-start.14
  49.5 0.1 convert_reduce_fusion
  49.6 0.1 reduce_max.9
  49.8 0.7 fusion.4
  51.2 8.9 %collective-permute-start.13 = (f32[32,2560]{1,0:T(8,128)S(1)}, f32[32,2560]{1,0:T(8,128)S(1)}, u32[]{:S(2)}, u32[]{:S(2)}) collective-permute-start(f32[32,2560]{1,0:T(8,128)S(1)} %get-tuple-element.71), channel_id=1, source_target_pairs={{0,8},{8,0},{16,24},{24,16},{1,9},{9,1},{17,25},{25,17},{2,10},{10... | collective-permute-start | bytes 983048 | tf_op jit(solution)/shard_map/ppermute | solution.py:343
  60.1 0.7 collective-permute-start.12
  60.9 1.6 collective-permute-start.16
  62.4 2.0 %slot_product.13 = (f32[4,32,1280]{2,1,0:T(8,128)S(1)}, f32[4,32,1280]{2,1,0:T(8,128)S(1)}) custom-call(s32[48]{0:T(128)S(1)} %reshape.75.meta_ref, f32[5120,2560]{1,0:T(8,128)} %a_ref.11, bf16[2560,256]{1,0:T(8,128)(2,1)S(1)} %copy-done.5, bf16[2560,256]{1,0:T(8,128)(2,1)} %copy-done.6, f32[4,32,1280]{2,1,0:T(8,128)S(1)} %collective-permute-done.15.refs_0_, ...), custom_call_target="tpu_custom_call" | custom-call | bytes 13107200 | tf_op jit(solution)/shard_map/slot_product/pallas_call | solution.py:166
  64.5 0.6 collective-permute-start.21
  65.1 6.4 %collective-permute-done.16.refs_1_ = f32[2,32,1280]{2,1,0:T(8,128)S(1)} collective-permute-done((f32[2,32,1280]{2,1,0:T(8,128)S(1)}, f32[2,32,1280]{2,1,0:T(8,128)S(1)}, u32[]{:S(2)}, u32[]{:S(2)}) %collective-permute-start.16) | collective-permute-done | bytes 327712 | tf_op jit(solution)/shard_map/ppermute | solution.py:379
  71.6 2.6 %collective-permute-start.26 = (f32[1,32,1280]{2,1,0:T(8,128)S(1)}, f32[1,32,1280]{2,1,0:T(8,128)S(1)}, u32[]{:S(2)}, u32[]{:S(2)}) collective-permute-start(f32[1,32,1280]{2,1,0:T(8,128)S(1)} %get-tuple-element.103), channel_id=1, source_target_pairs={{0,4},{1,5},{2,6},{3,7},{4,0},{5,1},{6,2},{7,3},{8,12},{9,13},{10,... | collective-permute-start | bytes 491528 | tf_op jit(solution)/shard_map/ppermute | solution.py:379
  74.2 2.7 %prepare_factor.3 = (bf16[2560,256]{1,0:T(8,128)(2,1)S(1)}, bf16[2560,256]{1,0:T(8,128)(2,1)S(1)}) custom-call(s32[48]{0:T(128)S(1)} %reshape.75.meta_ref, f32[64,2560]{1,0:T(8,128)} %get-tuple-element.69.refs_0_, f32[64,2560]{1,0:T(8,128)S(1)} %collective-permute-done.10.first.refs_1_, f32[64,2560]{1,0:T(8,128)S(1)} %collective-permute-done.11.second.refs_2_, ...), custom_call_target="tpu_custom_call" | custom-call | bytes 1024 | tf_op jit(solution)/shard_map/prepare_factor/pallas_call | solution.py:90
  76.9 9.0 %slot_product.12 = (f32[4,32,1280]{2,1,0:T(8,128)S(1)}, f32[4,32,1280]{2,1,0:T(8,128)S(1)}) custom-call(s32[48]{0:T(128)S(1)} %reshape.75.meta_ref, f32[5120,2560]{1,0:T(8,128)} %a_ref.11, bf16[2560,256]{1,0:T(8,128)(2,1)S(1)} %get-tuple-element.72.high_ref, bf16[2560,256]{1,0:T(8,128)(2,1)S(1)} %get-tuple-element.73.low_ref, ...), custom_call_target="tpu_custom_call" | custom-call | bytes 13107200 | tf_op jit(solution)/shard_map/slot_product/pallas_call | solution.py:166
  86.0 1.6 collective-permute-start.25
  87.7 0.4 collective-permute-start.30
  88.2 9.2 %slot_product.14 = (f32[4,32,1280]{2,1,0:T(8,128)S(1)}, f32[4,32,1280]{2,1,0:T(8,128)S(1)}) custom-call(s32[48]{0:T(128)S(1)} %reshape.75.meta_ref, f32[5120,2560]{1,0:T(8,128)} %a_ref.11, bf16[2560,256]{1,0:T(8,128)(2,1)S(1)} %get-tuple-element.72.high_ref, bf16[2560,256]{1,0:T(8,128)(2,1)S(1)} %get-tuple-element.73.low_ref, ...), custom_call_target="tpu_custom_call" | custom-call | bytes 13107200 | tf_op jit(solution)/shard_map/slot_product/pallas_call | solution.py:166
  97.4 2.3 %collective-permute-done.25.refs_1_ = f32[2,32,1280]{2,1,0:T(8,128)S(1)} collective-permute-done((f32[2,32,1280]{2,1,0:T(8,128)S(1)}, f32[2,32,1280]{2,1,0:T(8,128)S(1)}, u32[]{:S(2)}, u32[]{:S(2)}) %collective-permute-start.25) | collective-permute-done | bytes 327712 | tf_op jit(solution)/shard_map/ppermute | solution.py:379
  99.8 0.4 collective-permute-start.31
  100.2 1.7 collective-permute-start.18
  101.9 9.0 %slot_product.15 = (f32[4,32,1280]{2,1,0:T(8,128)S(1)}, f32[4,32,1280]{2,1,0:T(8,128)S(1)}) custom-call(s32[48]{0:T(128)S(1)} %reshape.75.meta_ref, f32[5120,2560]{1,0:T(8,128)} %a_ref.11, bf16[2560,256]{1,0:T(8,128)(2,1)S(1)} %get-tuple-element.72.high_ref, bf16[2560,256]{1,0:T(8,128)(2,1)S(1)} %get-tuple-element.73.low_ref, ...), custom_call_target="tpu_custom_call" | custom-call | bytes 13107200 | tf_op jit(solution)/shard_map/slot_product/pallas_call | solution.py:166
  111.0 0.5 collective-permute-start.23
  111.5 2.1 %collective-permute-done.18 = f32[2,32,1280]{2,1,0:T(8,128)S(1)} collective-permute-done((f32[2,32,1280]{2,1,0:T(8,128)S(1)}, f32[2,32,1280]{2,1,0:T(8,128)S(1)}, u32[]{:S(2)}, u32[]{:S(2)}) %collective-permute-start.18) | collective-permute-done | bytes 327712 | tf_op jit(solution)/shard_map/ppermute | solution.py:379
  113.6 0.6 collective-permute-start.19
  114.3 1.4 collective-permute-start.28
  115.7 9.4 %collective-permute-done.23 = f32[2,32,1280]{2,1,0:T(8,128)S(1)} collective-permute-done((f32[2,32,1280]{2,1,0:T(8,128)S(1)}, f32[2,32,1280]{2,1,0:T(8,128)S(1)}, u32[]{:S(2)}, u32[]{:S(2)}) %collective-permute-start.23) | collective-permute-done | bytes 327712 | tf_op jit(solution)/shard_map/ppermute | solution.py:379
  125.2 0.6 collective-permute-start.24
  125.8 9.5 %collective-permute-done.28 = f32[2,32,1280]{2,1,0:T(8,128)S(1)} collective-permute-done((f32[2,32,1280]{2,1,0:T(8,128)S(1)}, f32[2,32,1280]{2,1,0:T(8,128)S(1)}, u32[]{:S(2)}, u32[]{:S(2)}) %collective-permute-start.28) | collective-permute-done | bytes 327712 | tf_op jit(solution)/shard_map/ppermute | solution.py:379
  135.3 0.7 collective-permute-start.29
  136.0 1.5 place_slots.2
  137.5 2.4 %collective-permute-start.36 = (f32[32,1280]{1,0:T(8,128)S(1)}, f32[32,1280]{1,0:T(8,128)S(1)}, u32[]{:S(2)}, u32[]{:S(2)}) collective-permute-start(f32[32,1280]{1,0:T(8,128)S(1)} %get-tuple-element.94), channel_id=1, source_target_pairs={{0,2},{1,3},{2,0},{3,1},{4,6},{5,7},{6,4},{7,5},{8,10},{9,11},{10,... | collective-permute-start | bytes 491528 | tf_op jit(solution)/shard_map/ppermute | solution.py:379
  140.7 2.3 %collective-permute-start.38 = (f32[32,1280]{1,0:T(8,128)S(1)}, f32[32,1280]{1,0:T(8,128)S(1)}, u32[]{:S(2)}, u32[]{:S(2)}) collective-permute-start(f32[32,1280]{1,0:T(8,128)S(1)} %get-tuple-element.96), channel_id=1, source_target_pairs={{0,6},{1,7},{2,4},{3,5},{4,2},{5,3},{6,0},{7,1},{8,14},{9,15},{10,... | collective-permute-start | bytes 491528 | tf_op jit(solution)/shard_map/ppermute | solution.py:379
  143.1 3.5 %collective-permute-done.29.refs_5_ = f32[1,32,1280]{2,1,0:T(8,128)S(1)} collective-permute-done((f32[1,32,1280]{2,1,0:T(8,128)S(1)}, f32[1,32,1280]{2,1,0:T(8,128)S(1)}, u32[]{:S(2)}, u32[]{:S(2)}) %collective-permute-start.29) | collective-permute-done | bytes 163872 | tf_op jit(solution)/shard_map/ppermute | solution.py:379
  146.5 1.7 place_slots.3
  148.2 2.7 %collective-permute-start.33 = (f32[32,1280]{1,0:T(8,128)S(1)}, f32[32,1280]{1,0:T(8,128)S(1)}, u32[]{:S(2)}, u32[]{:S(2)}) collective-permute-start(f32[32,1280]{1,0:T(8,128)S(1)} %get-tuple-element.91), channel_id=1, source_target_pairs={{0,4},{1,5},{2,6},{3,7},{4,0},{5,1},{6,2},{7,3},{8,12},{9,13},{10,... | collective-permute-start | bytes 491528 | tf_op jit(solution)/shard_map/ppermute | solution.py:379
  150.9 1.7 collective-permute-start.34
  152.6 4.5 %collective-permute-done.37.refs_2_ = f32[32,1280]{1,0:T(8,128)S(1)} collective-permute-done((f32[32,1280]{1,0:T(8,128)S(1)}, f32[32,1280]{1,0:T(8,128)S(1)}, u32[]{:S(2)}, u32[]{:S(2)}) %collective-permute-start.37) | collective-permute-done | bytes 163872 | tf_op jit(solution)/shard_map/ppermute | solution.py:379
  157.2 3.1 %collective-permute-done.32.refs_1_ = f32[32,1280]{1,0:T(8,128)S(1)} collective-permute-done((f32[32,1280]{1,0:T(8,128)S(1)}, f32[32,1280]{1,0:T(8,128)S(1)}, u32[]{:S(2)}, u32[]{:S(2)}) %collective-permute-start.32) | collective-permute-done | bytes 163872 | tf_op jit(solution)/shard_map/ppermute | solution.py:379
  160.3 9.8 %collective-permute-done.33.refs_2_ = f32[32,1280]{1,0:T(8,128)S(1)} collective-permute-done((f32[32,1280]{1,0:T(8,128)S(1)}, f32[32,1280]{1,0:T(8,128)S(1)}, u32[]{:S(2)}, u32[]{:S(2)}) %collective-permute-start.33) | collective-permute-done | bytes 163872 | tf_op jit(solution)/shard_map/ppermute | solution.py:379
  170.3 1.2 place_panel.2.refs_5_
  171.5 0.5 collective-permute-done.35.refs_4_
  171.9 1.1 place_panel.3
  (75 shorter events, 1.6 us)
Async XLA Ops:
  0.6 1.3 copy-start
  1.9 4.6 %copy-start.7 = (s32[2,8]{1,0:T(2,128)S(1)}, s32[2,8]{1,0:T(2,128)}, u32[]{:S(2)}) copy-start(s32[2,8]{1,0:T(2,128)} %param.9) | copy-start | bytes 196
  1.9 29.1 %copy-start.1 = (f32[2,64,2560]{2,1,0:T(8,128)S(1)}, f32[2,64,2560]{2,1,0:T(8,128)}, u32[]{:S(2)}) copy-start(f32[2,64,2560]{2,1,0:T(8,128)} %refs_5_.1) | copy-start | bytes 3932164
  2.0 17.8 %collective-permute-start.7 = (f32[64,2560]{1,0:T(8,128)S(1)}, f32[64,2560]{1,0:T(8,128)S(1)}, u32[]{:S(2)}, u32[]{:S(2)}) collective-permute-start(f32[64,2560]{1,0:T(8,128)S(1)} %own_share.1.refs_0_), channel_id=1, source_target_pairs={{0,16},{8,24},{16,0},{24,8},{1,17},{9,25},{17,1},{25,9},{2,18},{10... | collective-permute-start | bytes 1966088 | tf_op jit(solution)/shard_map/ppermute | solution.py:343
  5.0 16.2 %collective-permute-start.6 = (f32[64,2560]{1,0:T(8,128)S(1)}, f32[64,2560]{1,0:T(8,128)S(1)}, u32[]{:S(2)}, u32[]{:S(2)}) collective-permute-start(f32[64,2560]{1,0:T(8,128)S(1)} %own_share.1.refs_0_), channel_id=1, source_target_pairs={{0,8},{8,0},{16,24},{24,16},{1,9},{9,1},{17,25},{25,17},{2,10},{10... | collective-permute-start | bytes 1966088 | tf_op jit(solution)/shard_map/ppermute | solution.py:343
  22.1 8.6 %collective-permute-start.8 = (f32[32,2560]{1,0:T(8,128)}, f32[32,2560]{1,0:T(8,128)}, u32[]{:S(2)}, u32[]{:S(2)}) collective-permute-start(f32[32,2560]{1,0:T(8,128)} %get-tuple-element.67), channel_id=1, source_target_pairs={{0,16},{8,24},{16,0},{24,8},{1,17},{9,25},{17,1},{25,9},{2,18},{10... | collective-permute-start | bytes 983048 | tf_op jit(solution)/shard_map/ppermute | solution.py:343
  22.5 8.6 %collective-permute-start.9 = (f32[32,2560]{1,0:T(8,128)}, f32[32,2560]{1,0:T(8,128)}, u32[]{:S(2)}, u32[]{:S(2)}) collective-permute-start(f32[32,2560]{1,0:T(8,128)} %get-tuple-element.68), channel_id=1, source_target_pairs={{0,8},{8,0},{16,24},{24,16},{1,9},{9,1},{17,25},{25,17},{2,10},{10... | collective-permute-start | bytes 983048 | tf_op jit(solution)/shard_map/ppermute | solution.py:343
  34.6 12.8 %copy-start.4 = (bf16[2560,256]{1,0:T(8,128)(2,1)}, bf16[2560,256]{1,0:T(8,128)(2,1)S(1)}, u32[]{:S(2)}) copy-start(bf16[2560,256]{1,0:T(8,128)(2,1)S(1)} %get-tuple-element.74.high_ref) | copy-start | bytes 3932164
  34.6 12.8 %copy-start.6 = (bf16[2560,256]{1,0:T(8,128)(2,1)}, bf16[2560,256]{1,0:T(8,128)(2,1)S(1)}, u32[]{:S(2)}) copy-start(bf16[2560,256]{1,0:T(8,128)(2,1)S(1)} %get-tuple-element.75.low_ref) | copy-start | bytes 3932164
  34.6 16.5 %collective-permute-start.11 = (f32[64,2560]{1,0:T(8,128)}, f32[64,2560]{1,0:T(8,128)S(1)}, u32[]{:S(2)}, u32[]{:S(2)}) collective-permute-start(f32[64,2560]{1,0:T(8,128)} %get-tuple-element.69.refs_0_), channel_id=1, source_target_pairs={{0,16},{8,24},{16,0},{24,8},{1,17},{9,25},{17,1},{25,9},{2,18},{10... | collective-permute-start | bytes 1966088 | tf_op jit(solution)/shard_map/ppermute | solution.py:343
  35.9 15.2 %collective-permute-start.10 = (f32[64,2560]{1,0:T(8,128)}, f32[64,2560]{1,0:T(8,128)S(1)}, u32[]{:S(2)}, u32[]{:S(2)}) collective-permute-start(f32[64,2560]{1,0:T(8,128)} %get-tuple-element.69.refs_0_), channel_id=1, source_target_pairs={{0,8},{8,0},{16,24},{24,16},{1,9},{9,1},{17,25},{25,17},{2,10},{10... | collective-permute-start | bytes 1966088 | tf_op jit(solution)/shard_map/ppermute | solution.py:343
  47.3 1.6 copy-start.2
  47.3 13.5 %collective-permute-start.15 = (f32[4,32,1280]{2,1,0:T(8,128)}, f32[4,32,1280]{2,1,0:T(8,128)S(1)}, u32[]{:S(2)}, u32[]{:S(2)}) collective-permute-start(f32[4,32,1280]{2,1,0:T(8,128)} %get-tuple-element.78), channel_id=1, source_target_pairs={{0,1},{1,0},{2,3},{3,2},{4,5},{5,4},{6,7},{7,6},{8,9},{9,8},{10,11... | collective-permute-start | bytes 1966088 | tf_op jit(solution)/shard_map/ppermute | solution.py:379
  48.9 15.5 %collective-permute-start.14 = (f32[4,32,1280]{2,1,0:T(8,128)}, f32[4,32,1280]{2,1,0:T(8,128)S(1)}, u32[]{:S(2)}, u32[]{:S(2)}) collective-permute-start(f32[4,32,1280]{2,1,0:T(8,128)} %get-tuple-element.76), channel_id=1, source_target_pairs={{0,1},{1,0},{2,3},{3,2},{4,5},{5,4},{6,7},{7,6},{8,9},{9,8},{10,11... | collective-permute-start | bytes 1966088 | tf_op jit(solution)/shard_map/ppermute | solution.py:379
  51.1 9.7 %copy-start.3 = (f32[4,32,1280]{2,1,0:T(8,128)S(1)}, f32[4,32,1280]{2,1,0:T(8,128)}, u32[]{:S(2)}) copy-start(f32[4,32,1280]{2,1,0:T(8,128)} %copy-done.2) | copy-start | bytes 1966084
  51.1 11.3 %copy-start.5 = (bf16[2560,256]{1,0:T(8,128)(2,1)S(1)}, bf16[2560,256]{1,0:T(8,128)(2,1)}, u32[]{:S(2)}) copy-start(bf16[2560,256]{1,0:T(8,128)(2,1)} %copy-done.4) | copy-start | bytes 3932164
  51.2 23.0 %collective-permute-start.13 = (f32[32,2560]{1,0:T(8,128)S(1)}, f32[32,2560]{1,0:T(8,128)S(1)}, u32[]{:S(2)}, u32[]{:S(2)}) collective-permute-start(f32[32,2560]{1,0:T(8,128)S(1)} %get-tuple-element.71), channel_id=1, source_target_pairs={{0,8},{8,0},{16,24},{24,16},{1,9},{9,1},{17,25},{25,17},{2,10},{10... | collective-permute-start | bytes 983048 | tf_op jit(solution)/shard_map/ppermute | solution.py:343
  60.1 14.1 %collective-permute-start.12 = (f32[32,2560]{1,0:T(8,128)S(1)}, f32[32,2560]{1,0:T(8,128)S(1)}, u32[]{:S(2)}, u32[]{:S(2)}) collective-permute-start(f32[32,2560]{1,0:T(8,128)S(1)} %get-tuple-element.70.refs_1_), channel_id=1, source_target_pairs={{0,16},{8,24},{16,0},{24,8},{1,17},{9,25},{17,1},{25,9},{2,18},{10... | collective-permute-start | bytes 983048 | tf_op jit(solution)/shard_map/ppermute | solution.py:343
  60.9 10.7 %collective-permute-start.16 = (f32[2,32,1280]{2,1,0:T(8,128)S(1)}, f32[2,32,1280]{2,1,0:T(8,128)S(1)}, u32[]{:S(2)}, u32[]{:S(2)}) collective-permute-start(f32[2,32,1280]{2,1,0:T(8,128)S(1)} %slice_add_fusion.15), channel_id=1, source_target_pairs={{0,2},{1,3},{2,0},{3,1},{4,6},{5,7},{6,4},{7,5},{8,10},{9,11},{10,... | collective-permute-start | bytes 983048 | tf_op jit(solution)/shard_map/ppermute | solution.py:379
  64.4 21.6 %collective-permute-start.20 = (f32[4,32,1280]{2,1,0:T(8,128)S(1)}, f32[4,32,1280]{2,1,0:T(8,128)S(1)}, u32[]{:S(2)}, u32[]{:S(2)}) collective-permute-start(f32[4,32,1280]{2,1,0:T(8,128)S(1)} %get-tuple-element.81), channel_id=1, source_target_pairs={{0,1},{1,0},{2,3},{3,2},{4,5},{5,4},{6,7},{7,6},{8,9},{9,8},{10,11... | collective-permute-start | bytes 1966088 | tf_op jit(solution)/shard_map/ppermute | solution.py:379
  64.5 23.2 %collective-permute-start.21 = (f32[2,32,1280]{2,1,0:T(8,128)S(1)}, f32[2,32,1280]{2,1,0:T(8,128)S(1)}, u32[]{:S(2)}, u32[]{:S(2)}) collective-permute-start(f32[2,32,1280]{2,1,0:T(8,128)S(1)} %slice_add_fusion.13), channel_id=1, source_target_pairs={{0,2},{1,3},{2,0},{3,1},{4,6},{5,7},{6,4},{7,5},{8,10},{9,11},{10,... | collective-permute-start | bytes 983048 | tf_op jit(solution)/shard_map/ppermute | solution.py:379
  71.6 30.3 %collective-permute-start.26 = (f32[1,32,1280]{2,1,0:T(8,128)S(1)}, f32[1,32,1280]{2,1,0:T(8,128)S(1)}, u32[]{:S(2)}, u32[]{:S(2)}) collective-permute-start(f32[1,32,1280]{2,1,0:T(8,128)S(1)} %get-tuple-element.103), channel_id=1, source_target_pairs={{0,4},{1,5},{2,6},{3,7},{4,0},{5,1},{6,2},{7,3},{8,12},{9,13},{10,... | collective-permute-start | bytes 491528 | tf_op jit(solution)/shard_map/ppermute | solution.py:379
  85.9 14.2 %collective-permute-start.17 = (f32[4,32,1280]{2,1,0:T(8,128)S(1)}, f32[4,32,1280]{2,1,0:T(8,128)S(1)}, u32[]{:S(2)}, u32[]{:S(2)}) collective-permute-start(f32[4,32,1280]{2,1,0:T(8,128)S(1)} %get-tuple-element.80), channel_id=1, source_target_pairs={{0,1},{1,0},{2,3},{3,2},{4,5},{5,4},{6,7},{7,6},{8,9},{9,8},{10,11... | collective-permute-start | bytes 1966088 | tf_op jit(solution)/shard_map/ppermute | solution.py:379
  86.0 13.7 %collective-permute-start.25 = (f32[2,32,1280]{2,1,0:T(8,128)S(1)}, f32[2,32,1280]{2,1,0:T(8,128)S(1)}, u32[]{:S(2)}, u32[]{:S(2)}) collective-permute-start(f32[2,32,1280]{2,1,0:T(8,128)S(1)} %slice_add_fusion.11), channel_id=1, source_target_pairs={{0,2},{1,3},{2,0},{3,1},{4,6},{5,7},{6,4},{7,5},{8,10},{9,11},{10,... | collective-permute-start | bytes 983048 | tf_op jit(solution)/shard_map/ppermute | solution.py:379
  87.7 48.2 %collective-permute-start.30 = (f32[1,32,1280]{2,1,0:T(8,128)S(1)}, f32[1,32,1280]{2,1,0:T(8,128)S(1)}, u32[]{:S(2)}, u32[]{:S(2)}) collective-permute-start(f32[1,32,1280]{2,1,0:T(8,128)S(1)} %get-tuple-element.100), channel_id=1, source_target_pairs={{0,4},{1,5},{2,6},{3,7},{4,0},{5,1},{6,2},{7,3},{8,12},{9,13},{10,... | collective-permute-start | bytes 491528 | tf_op jit(solution)/shard_map/ppermute | solution.py:379
  97.3 13.6 %collective-permute-start.22 = (f32[4,32,1280]{2,1,0:T(8,128)S(1)}, f32[4,32,1280]{2,1,0:T(8,128)S(1)}, u32[]{:S(2)}, u32[]{:S(2)}) collective-permute-start(f32[4,32,1280]{2,1,0:T(8,128)S(1)} %get-tuple-element.84), channel_id=1, source_target_pairs={{0,1},{1,0},{2,3},{3,2},{4,5},{5,4},{6,7},{7,6},{8,9},{9,8},{10,11... | collective-permute-start | bytes 1966088 | tf_op jit(solution)/shard_map/ppermute | solution.py:379
  99.8 36.2 %collective-permute-start.31 = (f32[1,32,1280]{2,1,0:T(8,128)S(1)}, f32[1,32,1280]{2,1,0:T(8,128)S(1)}, u32[]{:S(2)}, u32[]{:S(2)}) collective-permute-start(f32[1,32,1280]{2,1,0:T(8,128)S(1)} %get-tuple-element.98), channel_id=1, source_target_pairs={{0,4},{1,5},{2,6},{3,7},{4,0},{5,1},{6,2},{7,3},{8,12},{9,13},{10,... | collective-permute-start | bytes 491528 | tf_op jit(solution)/shard_map/ppermute | solution.py:379
  100.2 13.4 %collective-permute-start.18 = (f32[2,32,1280]{2,1,0:T(8,128)S(1)}, f32[2,32,1280]{2,1,0:T(8,128)S(1)}, u32[]{:S(2)}, u32[]{:S(2)}) collective-permute-start(f32[2,32,1280]{2,1,0:T(8,128)S(1)} %slice_add_fusion.14), channel_id=1, source_target_pairs={{0,2},{1,3},{2,0},{3,1},{4,6},{5,7},{6,4},{7,5},{8,10},{9,11},{10,... | collective-permute-start | bytes 983048 | tf_op jit(solution)/shard_map/ppermute | solution.py:379
  110.9 3.4 %collective-permute-start.27 = (f32[4,32,1280]{2,1,0:T(8,128)S(1)}, f32[4,32,1280]{2,1,0:T(8,128)S(1)}, u32[]{:S(2)}, u32[]{:S(2)}) collective-permute-start(f32[4,32,1280]{2,1,0:T(8,128)S(1)} %get-tuple-element.87), channel_id=1, source_target_pairs={{0,1},{1,0},{2,3},{3,2},{4,5},{5,4},{6,7},{7,6},{8,9},{9,8},{10,11... | collective-permute-start | bytes 1966088 | tf_op jit(solution)/shard_map/ppermute | solution.py:379
  111.0 14.1 %collective-permute-start.23 = (f32[2,32,1280]{2,1,0:T(8,128)S(1)}, f32[2,32,1280]{2,1,0:T(8,128)S(1)}, u32[]{:S(2)}, u32[]{:S(2)}) collective-permute-start(f32[2,32,1280]{2,1,0:T(8,128)S(1)} %slice_add_fusion.12), channel_id=1, source_target_pairs={{0,2},{1,3},{2,0},{3,1},{4,6},{5,7},{6,4},{7,5},{8,10},{9,11},{10,... | collective-permute-start | bytes 983048 | tf_op jit(solution)/shard_map/ppermute | solution.py:379
  113.6 27.1 %collective-permute-start.19 = (f32[1,32,1280]{2,1,0:T(8,128)S(1)}, f32[1,32,1280]{2,1,0:T(8,128)S(1)}, u32[]{:S(2)}, u32[]{:S(2)}) collective-permute-start(f32[1,32,1280]{2,1,0:T(8,128)S(1)} %get-tuple-element.108), channel_id=1, source_target_pairs={{0,4},{1,5},{2,6},{3,7},{4,0},{5,1},{6,2},{7,3},{8,12},{9,13},{10,... | collective-permute-start | bytes 491528 | tf_op jit(solution)/shard_map/ppermute | solution.py:379
  114.3 20.9 %collective-permute-start.28 = (f32[2,32,1280]{2,1,0:T(8,128)S(1)}, f32[2,32,1280]{2,1,0:T(8,128)S(1)}, u32[]{:S(2)}, u32[]{:S(2)}) collective-permute-start(f32[2,32,1280]{2,1,0:T(8,128)S(1)} %slice_add_fusion.10), channel_id=1, source_target_pairs={{0,2},{1,3},{2,0},{3,1},{4,6},{5,7},{6,4},{7,5},{8,10},{9,11},{10,... | collective-permute-start | bytes 983048 | tf_op jit(solution)/shard_map/ppermute | solution.py:379
  125.2 17.9 %collective-permute-start.24 = (f32[1,32,1280]{2,1,0:T(8,128)S(1)}, f32[1,32,1280]{2,1,0:T(8,128)S(1)}, u32[]{:S(2)}, u32[]{:S(2)}) collective-permute-start(f32[1,32,1280]{2,1,0:T(8,128)S(1)} %get-tuple-element.106), channel_id=1, source_target_pairs={{0,4},{1,5},{2,6},{3,7},{4,0},{5,1},{6,2},{7,3},{8,12},{9,13},{10,... | collective-permute-start | bytes 491528 | tf_op jit(solution)/shard_map/ppermute | solution.py:379
  135.3 11.2 %collective-permute-start.29 = (f32[1,32,1280]{2,1,0:T(8,128)S(1)}, f32[1,32,1280]{2,1,0:T(8,128)S(1)}, u32[]{:S(2)}, u32[]{:S(2)}) collective-permute-start(f32[1,32,1280]{2,1,0:T(8,128)S(1)} %get-tuple-element.104), channel_id=1, source_target_pairs={{0,4},{1,5},{2,6},{3,7},{4,0},{5,1},{6,2},{7,3},{8,12},{9,13},{10,... | collective-permute-start | bytes 491528 | tf_op jit(solution)/shard_map/ppermute | solution.py:379
  137.5 13.4 %collective-permute-start.36 = (f32[32,1280]{1,0:T(8,128)S(1)}, f32[32,1280]{1,0:T(8,128)S(1)}, u32[]{:S(2)}, u32[]{:S(2)}) collective-permute-start(f32[32,1280]{1,0:T(8,128)S(1)} %get-tuple-element.94), channel_id=1, source_target_pairs={{0,2},{1,3},{2,0},{3,1},{4,6},{5,7},{6,4},{7,5},{8,10},{9,11},{10,... | collective-permute-start | bytes 491528 | tf_op jit(solution)/shard_map/ppermute | solution.py:379
  140.6 16.5 %collective-permute-start.37 = (f32[32,1280]{1,0:T(8,128)S(1)}, f32[32,1280]{1,0:T(8,128)S(1)}, u32[]{:S(2)}, u32[]{:S(2)}) collective-permute-start(f32[32,1280]{1,0:T(8,128)S(1)} %get-tuple-element.95), channel_id=1, source_target_pairs={{0,4},{1,5},{2,6},{3,7},{4,0},{5,1},{6,2},{7,3},{8,12},{9,13},{10,... | collective-permute-start | bytes 491528 | tf_op jit(solution)/shard_map/ppermute | solution.py:379
  140.7 16.4 %collective-permute-start.38 = (f32[32,1280]{1,0:T(8,128)S(1)}, f32[32,1280]{1,0:T(8,128)S(1)}, u32[]{:S(2)}, u32[]{:S(2)}) collective-permute-start(f32[32,1280]{1,0:T(8,128)S(1)} %get-tuple-element.96), channel_id=1, source_target_pairs={{0,6},{1,7},{2,4},{3,5},{4,2},{5,3},{6,0},{7,1},{8,14},{9,15},{10,... | collective-permute-start | bytes 491528 | tf_op jit(solution)/shard_map/ppermute | solution.py:379
  148.2 12.1 %collective-permute-start.32 = (f32[32,1280]{1,0:T(8,128)S(1)}, f32[32,1280]{1,0:T(8,128)S(1)}, u32[]{:S(2)}, u32[]{:S(2)}) collective-permute-start(f32[32,1280]{1,0:T(8,128)S(1)} %get-tuple-element.90), channel_id=1, source_target_pairs={{0,2},{1,3},{2,0},{3,1},{4,6},{5,7},{6,4},{7,5},{8,10},{9,11},{10,... | collective-permute-start | bytes 491528 | tf_op jit(solution)/shard_map/ppermute | solution.py:379
  148.2 22.0 %collective-permute-start.33 = (f32[32,1280]{1,0:T(8,128)S(1)}, f32[32,1280]{1,0:T(8,128)S(1)}, u32[]{:S(2)}, u32[]{:S(2)}) collective-permute-start(f32[32,1280]{1,0:T(8,128)S(1)} %get-tuple-element.91), channel_id=1, source_target_pairs={{0,4},{1,5},{2,6},{3,7},{4,0},{5,1},{6,2},{7,3},{8,12},{9,13},{10,... | collective-permute-start | bytes 491528 | tf_op jit(solution)/shard_map/ppermute | solution.py:379
  150.9 19.3 %collective-permute-start.34 = (f32[32,1280]{1,0:T(8,128)S(1)}, f32[32,1280]{1,0:T(8,128)S(1)}, u32[]{:S(2)}, u32[]{:S(2)}) collective-permute-start(f32[32,1280]{1,0:T(8,128)S(1)} %get-tuple-element.92), channel_id=1, source_target_pairs={{0,6},{1,7},{2,4},{3,5},{4,2},{5,3},{6,0},{7,1},{8,14},{9,15},{10,... | collective-permute-start | bytes 491528 | tf_op jit(solution)/shard_map/ppermute | solution.py:379
  157.2 13.1 %collective-permute-start.39 = (f32[4,32,640]{2,1,0:T(8,128)S(1)}, f32[4,32,640]{2,1,0:T(8,128)S(1)}, u32[]{:S(2)}, u32[]{:S(2)}) collective-permute-start(f32[4,32,640]{2,1,0:T(8,128)S(1)} %split_halves.3), channel_id=1, source_target_pairs={{0,1},{1,0},{2,3},{3,2},{4,5},{5,4},{6,7},{7,6},{8,9},{9,8},{10,11... | collective-permute-start | bytes 983048 | tf_op jit(solution)/shard_map/ppermute | solution.py:379
  170.2 1.7 collective-permute-start.35
where the time goes:
time: 175 us; the launch traced here: 173 us
  waiting for transfers between devices  71.4 us (41%)
  Pallas kernels  53.3 us (30%)
  starting transfers between devices  41.9 us (24%)
  local copies, waits for them, and re-layouts  2.41 us (1%)
  between operations  2.28 us (1%)
    ppermute x26, waiting for transfers between devices, swap_col(): return lax.ppermute(value, 'col', [(c, c ^ flip) for c in range(count)])  51.1 us
    pallas_call x6, Pallas kernels, slot_product(): pl.pallas_call(functools.partial(slot_kernel, base, tile, len(after)), gr...  40.5 us
    ppermute x26, starting transfers between devices, swap_col(): return lax.ppermute(value, 'col', [(c, c ^ flip) for c in range(count)])  22.9 us
    ppermute x8, waiting for transfers between devices, swap(): return lax.ppermute(value, 'row', [(i, i ^ mask) for i in range(count)])  20.4 us
    ppermute x8, starting transfers between devices, swap(): return lax.ppermute(value, 'row', [(i, i ^ mask) for i in range(count)])  19 us
    pallas_call x2, Pallas kernels, prepare(): pl.pallas_call(functools.partial(prep_kernel, places, share, following is...  6.18 us
  transfers between devices with their start and end apart: 34, of which 14 were waited for; matrix products, arithmetic and copies ran while one was open for 2% of the time, Pallas kernels for 28%

commit v1 on v0

--- a/solution.py
+++ b/solution.py
@@ -457,8 +457,8 @@
 
     def exchange_of(placed):
         pieces = [placed[1]]
-        for flip in range(1, line):
-            pieces.append(swap_col(placed[1 + flip], 2 * flip, col_count))
+        for flip in range(line - 1, 0, -1):
+            pieces.insert(1, swap_col(placed[1 + flip], 2 * flip, col_count))
         return pieces
 
     done, parts, others, placed, pieces = [], [], [], [], []

time: 175 us -> 174 us (level)
  starting transfers between devices: 41.9 us -> 32.2 us
  Pallas kernels: 53.3 us -> 61.7 us
    ppermute x8, starting transfers between devices: 19 us -> 10.6 us  [swap(): return lax.ppermute(value, 'row', [(i, i ^ mask) for i in range(count)])]
    pallas_call x6, Pallas kernels: 40.5 us -> 48.9 us  [slot_product(): pl.pallas_call(functools.partial(slot_kernel, base, tile, len(after)), gr...]
  transfers between devices with their start and end apart: 34 -> 34, of which waited for: 14 -> 13; matrix products, arithmetic and copies ran while one was open for 2% -> 2% of each run, Pallas kernels for 28% -> 32%
where the time goes in v1:
time: 174 us; the launch traced here: 173 us
  waiting for transfers between devices  72.6 us (42%)
  Pallas kernels  61.7 us (35%)
  starting transfers between devices  32.2 us (19%)
  local copies, waits for them, and re-layouts  2.41 us (1%)
  between operations  2.32 us (1%)
    ppermute x26, waiting for transfers between devices, swap_col(): return lax.ppermute(value, 'col', [(c, c ^ flip) for c in range(count)])  52.2 us
    pallas_call x6, Pallas kernels, slot_product(): pl.pallas_call(functools.partial(slot_kernel, base, tile, len(after)), gr...  48.9 us
    ppermute x26, starting transfers between devices, swap_col(): return lax.ppermute(value, 'col', [(c, c ^ flip) for c in range(count)])  21.6 us
    ppermute x8, waiting for transfers between devices, swap(): return lax.ppermute(value, 'row', [(i, i ^ mask) for i in range(count)])  20.4 us
    ppermute x8, starting transfers between devices, swap(): return lax.ppermute(value, 'row', [(i, i ^ mask) for i in range(count)])  10.6 us
    pallas_call x2, Pallas kernels, prepare(): pl.pallas_call(functools.partial(prep_kernel, places, share, following is...  6.18 us
  transfers between devices with their start and end apart: 34, of which 13 were waited for; matrix products, arithmetic and copies ran while one was open for 2% of the time, Pallas kernels for 32%

profile of v1, /device:TPU:0, one launch (start us, length us, event | category | flops | bytes accessed | tf_op | source)
XLA Modules:
  0.0 172.9 jit_solution(9993511227233240844)
XLA Ops:
  0.6 1.3 copy-done
  2.0 3.0 %collective-permute-start.7 = (f32[64,2560]{1,0:T(8,128)S(1)}, f32[64,2560]{1,0:T(8,128)S(1)}, u32[]{:S(2)}, u32[]{:S(2)}) collective-permute-start(f32[64,2560]{1,0:T(8,128)S(1)} %own_share.1.refs_0_), channel_id=1, source_target_pairs={{0,16},{8,24},{16,0},{24,8},{1,17},{9,25},{17,1},{25,9},{2,18},{10... | collective-permute-start | bytes 1966088 | tf_op jit(solution)/shard_map/ppermute | solution.py:343
  5.0 1.5 collective-permute-start.6
  6.5 0.2 compare_reduce_fusion
  6.8 0.2 compare_reduce_fusion.1
  7.0 0.2 reduce_window_sum.11
  7.1 0.1 fusion.3
  7.3 12.5 %collective-permute-done.7.second.refs_2_ = f32[64,2560]{1,0:T(8,128)S(1)} collective-permute-done((f32[64,2560]{1,0:T(8,128)S(1)}, f32[64,2560]{1,0:T(8,128)S(1)}, u32[]{:S(2)}, u32[]{:S(2)}) %collective-permute-start.7) | collective-permute-done | bytes 655392 | tf_op jit(solution)/shard_map/ppermute | solution.py:343
  19.8 1.5 collective-permute-done.6.first.refs_1_
  21.2 0.9 relay_halves.2
  22.1 0.4 collective-permute-start.8
  22.5 1.6 collective-permute-start.9
  24.1 0.1 copy.10
  24.2 0.1 select_reduce_fusion
  24.3 0.1 copy.9
  24.5 0.1 concatenate.3
  24.6 0.1 reshape.75.meta_ref
  24.6 6.0 %collective-permute-done.8.refs_3_ = f32[32,2560]{1,0:T(8,128)} collective-permute-done((f32[32,2560]{1,0:T(8,128)}, f32[32,2560]{1,0:T(8,128)}, u32[]{:S(2)}, u32[]{:S(2)}) %collective-permute-start.8) | collective-permute-done | bytes 327712 | tf_op jit(solution)/shard_map/ppermute | solution.py:343
  30.7 0.4 collective-permute-done.9.refs_4_
  31.1 3.5 %prepare_factor.2 = (bf16[2560,256]{1,0:T(8,128)(2,1)S(1)}, bf16[2560,256]{1,0:T(8,128)(2,1)S(1)}, f32[64,2560]{1,0:T(8,128)}) custom-call(s32[48]{0:T(128)S(1)} %reshape.75.meta_ref, f32[64,2560]{1,0:T(8,128)S(1)} %own_share.1.refs_0_, f32[64,2560]{1,0:T(8,128)S(1)} %collective-permute-done.6.first.refs_1_, ...), custom_call_target="tpu_custom_call" | custom-call | bytes 1024 | tf_op jit(solution)/shard_map/prepare_factor/pallas_call | solution.py:90
  34.6 1.3 collective-permute-start.11
  35.9 1.5 collective-permute-start.10
  37.4 9.9 %slot_product.11 = (f32[4,32,1280]{2,1,0:T(8,128)S(1)}, f32[4,32,1280]{2,1,0:T(8,128)}) custom-call(s32[48]{0:T(128)S(1)} %reshape.75.meta_ref, f32[5120,2560]{1,0:T(8,128)} %a_ref.11, bf16[2560,256]{1,0:T(8,128)(2,1)S(1)} %get-tuple-element.74.high_ref, bf16[2560,256]{1,0:T(8,128)(2,1)S(1)} %get-tuple-element.75.low_ref), custom_call_target="tpu_custom_call" | custom-call | bytes 13107200 | tf_op jit(solution)/shard_map/slot_product/pallas_call | solution.py:166
  47.4 9.8 %slot_product.10 = (f32[4,32,1280]{2,1,0:T(8,128)S(1)}, f32[4,32,1280]{2,1,0:T(8,128)}) custom-call(s32[48]{0:T(128)S(1)} %reshape.75.meta_ref, f32[5120,2560]{1,0:T(8,128)} %a_ref.11, bf16[2560,256]{1,0:T(8,128)(2,1)S(1)} %get-tuple-element.74.high_ref, bf16[2560,256]{1,0:T(8,128)(2,1)S(1)} %get-tuple-element.75.low_ref), custom_call_target="tpu_custom_call" | custom-call | bytes 13107200 | tf_op jit(solution)/shard_map/slot_product/pallas_call | solution.py:166
  57.3 0.6 collective-permute-start.14
  57.8 0.1 convert_reduce_fusion
  58.0 0.1 reduce_max.9
  58.1 0.7 fusion.4
  59.6 1.2 collective-permute-start.12
  60.9 1.6 collective-permute-start.16
  62.4 10.3 %slot_product.13 = (f32[4,32,1280]{2,1,0:T(8,128)S(1)}, f32[4,32,1280]{2,1,0:T(8,128)S(1)}) custom-call(s32[48]{0:T(128)S(1)} %reshape.75.meta_ref, f32[5120,2560]{1,0:T(8,128)} %a_ref.11, bf16[2560,256]{1,0:T(8,128)(2,1)S(1)} %copy-done.5, bf16[2560,256]{1,0:T(8,128)(2,1)} %copy-done.6, f32[4,32,1280]{2,1,0:T(8,128)S(1)} %collective-permute-done.15.refs_0_, ...), custom_call_target="tpu_custom_call" | custom-call | bytes 13107200 | tf_op jit(solution)/shard_map/slot_product/pallas_call | solution.py:166
  72.9 0.6 collective-permute-start.21
  73.5 2.6 %collective-permute-start.26 = (f32[1,32,1280]{2,1,0:T(8,128)S(1)}, f32[1,32,1280]{2,1,0:T(8,128)S(1)}, u32[]{:S(2)}, u32[]{:S(2)}) collective-permute-start(f32[1,32,1280]{2,1,0:T(8,128)S(1)} %get-tuple-element.103), channel_id=1, source_target_pairs={{0,4},{1,5},{2,6},{3,7},{4,0},{5,1},{6,2},{7,3},{8,12},{9,13},{10,... | collective-permute-start | bytes 491528 | tf_op jit(solution)/shard_map/ppermute | solution.py:379
  76.1 2.7 %prepare_factor.3 = (bf16[2560,256]{1,0:T(8,128)(2,1)S(1)}, bf16[2560,256]{1,0:T(8,128)(2,1)S(1)}) custom-call(s32[48]{0:T(128)S(1)} %reshape.75.meta_ref, f32[64,2560]{1,0:T(8,128)} %get-tuple-element.69.refs_0_, f32[64,2560]{1,0:T(8,128)S(1)} %collective-permute-done.10.first.refs_1_, f32[64,2560]{1,0:T(8,128)S(1)} %collective-permute-done.11.second.refs_2_, ...), custom_call_target="tpu_custom_call" | custom-call | bytes 1024 | tf_op jit(solution)/shard_map/prepare_factor/pallas_call | solution.py:90
  78.8 9.0 %slot_product.12 = (f32[4,32,1280]{2,1,0:T(8,128)S(1)}, f32[4,32,1280]{2,1,0:T(8,128)S(1)}) custom-call(s32[48]{0:T(128)S(1)} %reshape.75.meta_ref, f32[5120,2560]{1,0:T(8,128)} %a_ref.11, bf16[2560,256]{1,0:T(8,128)(2,1)S(1)} %get-tuple-element.72.high_ref, bf16[2560,256]{1,0:T(8,128)(2,1)S(1)} %get-tuple-element.73.low_ref, ...), custom_call_target="tpu_custom_call" | custom-call | bytes 13107200 | tf_op jit(solution)/shard_map/slot_product/pallas_call | solution.py:166
  87.8 0.1 collective-permute-start.17
  87.9 1.7 collective-permute-start.25
  89.7 0.4 collective-permute-start.30
  90.1 9.2 %slot_product.14 = (f32[4,32,1280]{2,1,0:T(8,128)S(1)}, f32[4,32,1280]{2,1,0:T(8,128)S(1)}) custom-call(s32[48]{0:T(128)S(1)} %reshape.75.meta_ref, f32[5120,2560]{1,0:T(8,128)} %a_ref.11, bf16[2560,256]{1,0:T(8,128)(2,1)S(1)} %get-tuple-element.72.high_ref, bf16[2560,256]{1,0:T(8,128)(2,1)S(1)} %get-tuple-element.73.low_ref, ...), custom_call_target="tpu_custom_call" | custom-call | bytes 13107200 | tf_op jit(solution)/shard_map/slot_product/pallas_call | solution.py:166
  99.3 2.3 %collective-permute-done.25.refs_1_ = f32[2,32,1280]{2,1,0:T(8,128)S(1)} collective-permute-done((f32[2,32,1280]{2,1,0:T(8,128)S(1)}, f32[2,32,1280]{2,1,0:T(8,128)S(1)}, u32[]{:S(2)}, u32[]{:S(2)}) %collective-permute-start.25) | collective-permute-done | bytes 327712 | tf_op jit(solution)/shard_map/ppermute | solution.py:379
  101.7 0.4 collective-permute-start.31
  102.1 1.7 collective-permute-start.18
  103.8 0.7 slot_product.15
  104.4 0.1 collective-permute-start.27
  104.6 0.5 collective-permute-start.23
  105.1 11.1 %collective-permute-done.18 = f32[2,32,1280]{2,1,0:T(8,128)S(1)} collective-permute-done((f32[2,32,1280]{2,1,0:T(8,128)S(1)}, f32[2,32,1280]{2,1,0:T(8,128)S(1)}, u32[]{:S(2)}, u32[]{:S(2)}) %collective-permute-start.18) | collective-permute-done | bytes 327712 | tf_op jit(solution)/shard_map/ppermute | solution.py:379
  116.2 0.1 collective-permute-start.19
  116.4 2.0 %collective-permute-start.28 = (f32[2,32,1280]{2,1,0:T(8,128)S(1)}, f32[2,32,1280]{2,1,0:T(8,128)S(1)}, u32[]{:S(2)}, u32[]{:S(2)}) collective-permute-start(f32[2,32,1280]{2,1,0:T(8,128)S(1)} %slice_add_fusion.10), channel_id=1, source_target_pairs={{0,2},{1,3},{2,0},{3,1},{4,6},{5,7},{6,4},{7,5},{8,10},{9,11},{10,... | collective-permute-start | bytes 983048 | tf_op jit(solution)/shard_map/ppermute | solution.py:379
  118.4 8.3 %collective-permute-done.23 = f32[2,32,1280]{2,1,0:T(8,128)S(1)} collective-permute-done((f32[2,32,1280]{2,1,0:T(8,128)S(1)}, f32[2,32,1280]{2,1,0:T(8,128)S(1)}, u32[]{:S(2)}, u32[]{:S(2)}) %collective-permute-start.23) | collective-permute-done | bytes 327712 | tf_op jit(solution)/shard_map/ppermute | solution.py:379
  126.8 9.7 %collective-permute-done.28 = f32[2,32,1280]{2,1,0:T(8,128)S(1)} collective-permute-done((f32[2,32,1280]{2,1,0:T(8,128)S(1)}, f32[2,32,1280]{2,1,0:T(8,128)S(1)}, u32[]{:S(2)}, u32[]{:S(2)}) %collective-permute-start.28) | collective-permute-done | bytes 327712 | tf_op jit(solution)/shard_map/ppermute | solution.py:379
  136.7 1.7 place_slots.2
  138.4 1.9 %collective-permute-start.36 = (f32[32,1280]{1,0:T(8,128)S(1)}, f32[32,1280]{1,0:T(8,128)S(1)}, u32[]{:S(2)}, u32[]{:S(2)}) collective-permute-start(f32[32,1280]{1,0:T(8,128)S(1)} %get-tuple-element.94), channel_id=1, source_target_pairs={{0,2},{1,3},{2,0},{3,1},{4,6},{5,7},{6,4},{7,5},{8,10},{9,11},{10,... | collective-permute-start | bytes 491528 | tf_op jit(solution)/shard_map/ppermute | solution.py:379
  140.9 1.1 collective-permute-start.37
  142.0 1.5 collective-permute-start.38
  143.6 7.8 %collective-permute-done.29.refs_5_ = f32[1,32,1280]{2,1,0:T(8,128)S(1)} collective-permute-done((f32[1,32,1280]{2,1,0:T(8,128)S(1)}, f32[1,32,1280]{2,1,0:T(8,128)S(1)}, u32[]{:S(2)}, u32[]{:S(2)}) %collective-permute-start.29) | collective-permute-done | bytes 163872 | tf_op jit(solution)/shard_map/ppermute | solution.py:379
  151.4 1.6 place_slots.3
  153.0 3.3 %collective-permute-start.33 = (f32[32,1280]{1,0:T(8,128)S(1)}, f32[32,1280]{1,0:T(8,128)S(1)}, u32[]{:S(2)}, u32[]{:S(2)}) collective-permute-start(f32[32,1280]{1,0:T(8,128)S(1)} %get-tuple-element.91), channel_id=1, source_target_pairs={{0,4},{1,5},{2,6},{3,7},{4,0},{5,1},{6,2},{7,3},{8,12},{9,13},{10,... | collective-permute-start | bytes 491528 | tf_op jit(solution)/shard_map/ppermute | solution.py:379
  156.2 1.1 collective-permute-start.34
  157.4 2.1 %collective-permute-done.37.refs_2_ = f32[32,1280]{1,0:T(8,128)S(1)} collective-permute-done((f32[32,1280]{1,0:T(8,128)S(1)}, f32[32,1280]{1,0:T(8,128)S(1)}, u32[]{:S(2)}, u32[]{:S(2)}) %collective-permute-start.37) | collective-permute-done | bytes 163872 | tf_op jit(solution)/shard_map/ppermute | solution.py:379
  159.6 1.5 collective-permute-done.32.refs_1_
  161.1 8.9 %collective-permute-done.33.refs_2_ = f32[32,1280]{1,0:T(8,128)S(1)} collective-permute-done((f32[32,1280]{1,0:T(8,128)S(1)}, f32[32,1280]{1,0:T(8,128)S(1)}, u32[]{:S(2)}, u32[]{:S(2)}) %collective-permute-start.33) | collective-permute-done | bytes 163872 | tf_op jit(solution)/shard_map/ppermute | solution.py:379
  170.2 1.2 place_panel.2.refs_5_
  171.3 0.5 collective-permute-done.35.refs_4_
  171.8 1.1 place_panel.3
  (75 shorter events, 1.5 us)
Async XLA Ops:
  0.6 1.3 copy-start
  1.9 4.6 %copy-start.7 = (s32[2,8]{1,0:T(2,128)S(1)}, s32[2,8]{1,0:T(2,128)}, u32[]{:S(2)}) copy-start(s32[2,8]{1,0:T(2,128)} %param.9) | copy-start | bytes 196
  1.9 29.1 %copy-start.1 = (f32[2,64,2560]{2,1,0:T(8,128)S(1)}, f32[2,64,2560]{2,1,0:T(8,128)}, u32[]{:S(2)}) copy-start(f32[2,64,2560]{2,1,0:T(8,128)} %refs_5_.1) | copy-start | bytes 3932164
  2.0 17.8 %collective-permute-start.7 = (f32[64,2560]{1,0:T(8,128)S(1)}, f32[64,2560]{1,0:T(8,128)S(1)}, u32[]{:S(2)}, u32[]{:S(2)}) collective-permute-start(f32[64,2560]{1,0:T(8,128)S(1)} %own_share.1.refs_0_), channel_id=1, source_target_pairs={{0,16},{8,24},{16,0},{24,8},{1,17},{9,25},{17,1},{25,9},{2,18},{10... | collective-permute-start | bytes 1966088 | tf_op jit(solution)/shard_map/ppermute | solution.py:343
  5.0 16.2 %collective-permute-start.6 = (f32[64,2560]{1,0:T(8,128)S(1)}, f32[64,2560]{1,0:T(8,128)S(1)}, u32[]{:S(2)}, u32[]{:S(2)}) collective-permute-start(f32[64,2560]{1,0:T(8,128)S(1)} %own_share.1.refs_0_), channel_id=1, source_target_pairs={{0,8},{8,0},{16,24},{24,16},{1,9},{9,1},{17,25},{25,17},{2,10},{10... | collective-permute-start | bytes 1966088 | tf_op jit(solution)/shard_map/ppermute | solution.py:343
  22.1 8.6 %collective-permute-start.8 = (f32[32,2560]{1,0:T(8,128)}, f32[32,2560]{1,0:T(8,128)}, u32[]{:S(2)}, u32[]{:S(2)}) collective-permute-start(f32[32,2560]{1,0:T(8,128)} %get-tuple-element.67), channel_id=1, source_target_pairs={{0,16},{8,24},{16,0},{24,8},{1,17},{9,25},{17,1},{25,9},{2,18},{10... | collective-permute-start | bytes 983048 | tf_op jit(solution)/shard_map/ppermute | solution.py:343
  22.5 8.6 %collective-permute-start.9 = (f32[32,2560]{1,0:T(8,128)}, f32[32,2560]{1,0:T(8,128)}, u32[]{:S(2)}, u32[]{:S(2)}) collective-permute-start(f32[32,2560]{1,0:T(8,128)} %get-tuple-element.68), channel_id=1, source_target_pairs={{0,8},{8,0},{16,24},{24,16},{1,9},{9,1},{17,25},{25,17},{2,10},{10... | collective-permute-start | bytes 983048 | tf_op jit(solution)/shard_map/ppermute | solution.py:343
  34.6 12.8 %copy-start.4 = (bf16[2560,256]{1,0:T(8,128)(2,1)}, bf16[2560,256]{1,0:T(8,128)(2,1)S(1)}, u32[]{:S(2)}) copy-start(bf16[2560,256]{1,0:T(8,128)(2,1)S(1)} %get-tuple-element.74.high_ref) | copy-start | bytes 3932164
  34.6 12.8 %copy-start.6 = (bf16[2560,256]{1,0:T(8,128)(2,1)}, bf16[2560,256]{1,0:T(8,128)(2,1)S(1)}, u32[]{:S(2)}) copy-start(bf16[2560,256]{1,0:T(8,128)(2,1)S(1)} %get-tuple-element.75.low_ref) | copy-start | bytes 3932164
  34.6 24.9 %collective-permute-start.11 = (f32[64,2560]{1,0:T(8,128)}, f32[64,2560]{1,0:T(8,128)S(1)}, u32[]{:S(2)}, u32[]{:S(2)}) collective-permute-start(f32[64,2560]{1,0:T(8,128)} %get-tuple-element.69.refs_0_), channel_id=1, source_target_pairs={{0,16},{8,24},{16,0},{24,8},{1,17},{9,25},{17,1},{25,9},{2,18},{10... | collective-permute-start | bytes 1966088 | tf_op jit(solution)/shard_map/ppermute | solution.py:343
  35.9 23.5 %collective-permute-start.10 = (f32[64,2560]{1,0:T(8,128)}, f32[64,2560]{1,0:T(8,128)S(1)}, u32[]{:S(2)}, u32[]{:S(2)}) collective-permute-start(f32[64,2560]{1,0:T(8,128)} %get-tuple-element.69.refs_0_), channel_id=1, source_target_pairs={{0,8},{8,0},{16,24},{24,16},{1,9},{9,1},{17,25},{25,17},{2,10},{10... | collective-permute-start | bytes 1966088 | tf_op jit(solution)/shard_map/ppermute | solution.py:343
  47.3 10.0 %copy-start.2 = (f32[4,32,1280]{2,1,0:T(8,128)}, f32[4,32,1280]{2,1,0:T(8,128)S(1)}, u32[]{:S(2)}) copy-start(f32[4,32,1280]{2,1,0:T(8,128)S(1)} %get-tuple-element.77) | copy-start | bytes 1966084
  47.3 13.5 %collective-permute-start.15 = (f32[4,32,1280]{2,1,0:T(8,128)}, f32[4,32,1280]{2,1,0:T(8,128)S(1)}, u32[]{:S(2)}, u32[]{:S(2)}) collective-permute-start(f32[4,32,1280]{2,1,0:T(8,128)} %get-tuple-element.78), channel_id=1, source_target_pairs={{0,1},{1,0},{2,3},{3,2},{4,5},{5,4},{6,7},{7,6},{8,9},{9,8},{10,11... | collective-permute-start | bytes 1966088 | tf_op jit(solution)/shard_map/ppermute | solution.py:379
  57.3 15.5 %collective-permute-start.14 = (f32[4,32,1280]{2,1,0:T(8,128)}, f32[4,32,1280]{2,1,0:T(8,128)S(1)}, u32[]{:S(2)}, u32[]{:S(2)}) collective-permute-start(f32[4,32,1280]{2,1,0:T(8,128)} %get-tuple-element.76), channel_id=1, source_target_pairs={{0,1},{1,0},{2,3},{3,2},{4,5},{5,4},{6,7},{7,6},{8,9},{9,8},{10,11... | collective-permute-start | bytes 1966088 | tf_op jit(solution)/shard_map/ppermute | solution.py:379
  59.4 1.4 copy-start.3
  59.4 3.0 %copy-start.5 = (bf16[2560,256]{1,0:T(8,128)(2,1)S(1)}, bf16[2560,256]{1,0:T(8,128)(2,1)}, u32[]{:S(2)}) copy-start(bf16[2560,256]{1,0:T(8,128)(2,1)} %copy-done.4) | copy-start | bytes 3932164
  59.5 16.6 %collective-permute-start.13 = (f32[32,2560]{1,0:T(8,128)S(1)}, f32[32,2560]{1,0:T(8,128)S(1)}, u32[]{:S(2)}, u32[]{:S(2)}) collective-permute-start(f32[32,2560]{1,0:T(8,128)S(1)} %get-tuple-element.71), channel_id=1, source_target_pairs={{0,8},{8,0},{16,24},{24,16},{1,9},{9,1},{17,25},{25,17},{2,10},{10... | collective-permute-start | bytes 983048 | tf_op jit(solution)/shard_map/ppermute | solution.py:343
  59.6 16.5 %collective-permute-start.12 = (f32[32,2560]{1,0:T(8,128)S(1)}, f32[32,2560]{1,0:T(8,128)S(1)}, u32[]{:S(2)}, u32[]{:S(2)}) collective-permute-start(f32[32,2560]{1,0:T(8,128)S(1)} %get-tuple-element.70.refs_1_), channel_id=1, source_target_pairs={{0,16},{8,24},{16,0},{24,8},{1,17},{9,25},{17,1},{25,9},{2,18},{10... | collective-permute-start | bytes 983048 | tf_op jit(solution)/shard_map/ppermute | solution.py:343
  60.9 12.6 %collective-permute-start.16 = (f32[2,32,1280]{2,1,0:T(8,128)S(1)}, f32[2,32,1280]{2,1,0:T(8,128)S(1)}, u32[]{:S(2)}, u32[]{:S(2)}) collective-permute-start(f32[2,32,1280]{2,1,0:T(8,128)S(1)} %slice_add_fusion.15), channel_id=1, source_target_pairs={{0,2},{1,3},{2,0},{3,1},{4,6},{5,7},{6,4},{7,5},{8,10},{9,11},{10,... | collective-permute-start | bytes 983048 | tf_op jit(solution)/shard_map/ppermute | solution.py:379
  72.7 15.2 %collective-permute-start.20 = (f32[4,32,1280]{2,1,0:T(8,128)S(1)}, f32[4,32,1280]{2,1,0:T(8,128)S(1)}, u32[]{:S(2)}, u32[]{:S(2)}) collective-permute-start(f32[4,32,1280]{2,1,0:T(8,128)S(1)} %get-tuple-element.81), channel_id=1, source_target_pairs={{0,1},{1,0},{2,3},{3,2},{4,5},{5,4},{6,7},{7,6},{8,9},{9,8},{10,11... | collective-permute-start | bytes 1966088 | tf_op jit(solution)/shard_map/ppermute | solution.py:379
  72.9 16.7 %collective-permute-start.21 = (f32[2,32,1280]{2,1,0:T(8,128)S(1)}, f32[2,32,1280]{2,1,0:T(8,128)S(1)}, u32[]{:S(2)}, u32[]{:S(2)}) collective-permute-start(f32[2,32,1280]{2,1,0:T(8,128)S(1)} %slice_add_fusion.13), channel_id=1, source_target_pairs={{0,2},{1,3},{2,0},{3,1},{4,6},{5,7},{6,4},{7,5},{8,10},{9,11},{10,... | collective-permute-start | bytes 983048 | tf_op jit(solution)/shard_map/ppermute | solution.py:379
  73.5 30.3 %collective-permute-start.26 = (f32[1,32,1280]{2,1,0:T(8,128)S(1)}, f32[1,32,1280]{2,1,0:T(8,128)S(1)}, u32[]{:S(2)}, u32[]{:S(2)}) collective-permute-start(f32[1,32,1280]{2,1,0:T(8,128)S(1)} %get-tuple-element.103), channel_id=1, source_target_pairs={{0,4},{1,5},{2,6},{3,7},{4,0},{5,1},{6,2},{7,3},{8,12},{9,13},{10,... | collective-permute-start | bytes 491528 | tf_op jit(solution)/shard_map/ppermute | solution.py:379
  87.8 14.2 %collective-permute-start.17 = (f32[4,32,1280]{2,1,0:T(8,128)S(1)}, f32[4,32,1280]{2,1,0:T(8,128)S(1)}, u32[]{:S(2)}, u32[]{:S(2)}) collective-permute-start(f32[4,32,1280]{2,1,0:T(8,128)S(1)} %get-tuple-element.80), channel_id=1, source_target_pairs={{0,1},{1,0},{2,3},{3,2},{4,5},{5,4},{6,7},{7,6},{8,9},{9,8},{10,11... | collective-permute-start | bytes 1966088 | tf_op jit(solution)/shard_map/ppermute | solution.py:379
  87.9 13.7 %collective-permute-start.25 = (f32[2,32,1280]{2,1,0:T(8,128)S(1)}, f32[2,32,1280]{2,1,0:T(8,128)S(1)}, u32[]{:S(2)}, u32[]{:S(2)}) collective-permute-start(f32[2,32,1280]{2,1,0:T(8,128)S(1)} %slice_add_fusion.11), channel_id=1, source_target_pairs={{0,2},{1,3},{2,0},{3,1},{4,6},{5,7},{6,4},{7,5},{8,10},{9,11},{10,... | collective-permute-start | bytes 983048 | tf_op jit(solution)/shard_map/ppermute | solution.py:379
  89.7 47.0 %collective-permute-start.30 = (f32[1,32,1280]{2,1,0:T(8,128)S(1)}, f32[1,32,1280]{2,1,0:T(8,128)S(1)}, u32[]{:S(2)}, u32[]{:S(2)}) collective-permute-start(f32[1,32,1280]{2,1,0:T(8,128)S(1)} %get-tuple-element.100), channel_id=1, source_target_pairs={{0,4},{1,5},{2,6},{3,7},{4,0},{5,1},{6,2},{7,3},{8,12},{9,13},{10,... | collective-permute-start | bytes 491528 | tf_op jit(solution)/shard_map/ppermute | solution.py:379
  99.2 5.3 %collective-permute-start.22 = (f32[4,32,1280]{2,1,0:T(8,128)S(1)}, f32[4,32,1280]{2,1,0:T(8,128)S(1)}, u32[]{:S(2)}, u32[]{:S(2)}) collective-permute-start(f32[4,32,1280]{2,1,0:T(8,128)S(1)} %get-tuple-element.84), channel_id=1, source_target_pairs={{0,1},{1,0},{2,3},{3,2},{4,5},{5,4},{6,7},{7,6},{8,9},{9,8},{10,11... | collective-permute-start | bytes 1966088 | tf_op jit(solution)/shard_map/ppermute | solution.py:379
  101.7 35.0 %collective-permute-start.31 = (f32[1,32,1280]{2,1,0:T(8,128)S(1)}, f32[1,32,1280]{2,1,0:T(8,128)S(1)}, u32[]{:S(2)}, u32[]{:S(2)}) collective-permute-start(f32[1,32,1280]{2,1,0:T(8,128)S(1)} %get-tuple-element.98), channel_id=1, source_target_pairs={{0,4},{1,5},{2,6},{3,7},{4,0},{5,1},{6,2},{7,3},{8,12},{9,13},{10,... | collective-permute-start | bytes 491528 | tf_op jit(solution)/shard_map/ppermute | solution.py:379
  102.1 14.0 %collective-permute-start.18 = (f32[2,32,1280]{2,1,0:T(8,128)S(1)}, f32[2,32,1280]{2,1,0:T(8,128)S(1)}, u32[]{:S(2)}, u32[]{:S(2)}) collective-permute-start(f32[2,32,1280]{2,1,0:T(8,128)S(1)} %slice_add_fusion.14), channel_id=1, source_target_pairs={{0,2},{1,3},{2,0},{3,1},{4,6},{5,7},{6,4},{7,5},{8,10},{9,11},{10,... | collective-permute-start | bytes 983048 | tf_op jit(solution)/shard_map/ppermute | solution.py:379
  104.4 11.9 %collective-permute-start.27 = (f32[4,32,1280]{2,1,0:T(8,128)S(1)}, f32[4,32,1280]{2,1,0:T(8,128)S(1)}, u32[]{:S(2)}, u32[]{:S(2)}) collective-permute-start(f32[4,32,1280]{2,1,0:T(8,128)S(1)} %get-tuple-element.87), channel_id=1, source_target_pairs={{0,1},{1,0},{2,3},{3,2},{4,5},{5,4},{6,7},{7,6},{8,9},{9,8},{10,11... | collective-permute-start | bytes 1966088 | tf_op jit(solution)/shard_map/ppermute | solution.py:379
  104.6 22.1 %collective-permute-start.23 = (f32[2,32,1280]{2,1,0:T(8,128)S(1)}, f32[2,32,1280]{2,1,0:T(8,128)S(1)}, u32[]{:S(2)}, u32[]{:S(2)}) collective-permute-start(f32[2,32,1280]{2,1,0:T(8,128)S(1)} %slice_add_fusion.12), channel_id=1, source_target_pairs={{0,2},{1,3},{2,0},{3,1},{4,6},{5,7},{6,4},{7,5},{8,10},{9,11},{10,... | collective-permute-start | bytes 983048 | tf_op jit(solution)/shard_map/ppermute | solution.py:379
  116.2 25.8 %collective-permute-start.19 = (f32[1,32,1280]{2,1,0:T(8,128)S(1)}, f32[1,32,1280]{2,1,0:T(8,128)S(1)}, u32[]{:S(2)}, u32[]{:S(2)}) collective-permute-start(f32[1,32,1280]{2,1,0:T(8,128)S(1)} %get-tuple-element.108), channel_id=1, source_target_pairs={{0,4},{1,5},{2,6},{3,7},{4,0},{5,1},{6,2},{7,3},{8,12},{9,13},{10,... | collective-permute-start | bytes 491528 | tf_op jit(solution)/shard_map/ppermute | solution.py:379
  116.4 20.2 %collective-permute-start.28 = (f32[2,32,1280]{2,1,0:T(8,128)S(1)}, f32[2,32,1280]{2,1,0:T(8,128)S(1)}, u32[]{:S(2)}, u32[]{:S(2)}) collective-permute-start(f32[2,32,1280]{2,1,0:T(8,128)S(1)} %slice_add_fusion.10), channel_id=1, source_target_pairs={{0,2},{1,3},{2,0},{3,1},{4,6},{5,7},{6,4},{7,5},{8,10},{9,11},{10,... | collective-permute-start | bytes 983048 | tf_op jit(solution)/shard_map/ppermute | solution.py:379
  126.7 16.8 %collective-permute-start.24 = (f32[1,32,1280]{2,1,0:T(8,128)S(1)}, f32[1,32,1280]{2,1,0:T(8,128)S(1)}, u32[]{:S(2)}, u32[]{:S(2)}) collective-permute-start(f32[1,32,1280]{2,1,0:T(8,128)S(1)} %get-tuple-element.106), channel_id=1, source_target_pairs={{0,4},{1,5},{2,6},{3,7},{4,0},{5,1},{6,2},{7,3},{8,12},{9,13},{10,... | collective-permute-start | bytes 491528 | tf_op jit(solution)/shard_map/ppermute | solution.py:379
  136.6 14.8 %collective-permute-start.29 = (f32[1,32,1280]{2,1,0:T(8,128)S(1)}, f32[1,32,1280]{2,1,0:T(8,128)S(1)}, u32[]{:S(2)}, u32[]{:S(2)}) collective-permute-start(f32[1,32,1280]{2,1,0:T(8,128)S(1)} %get-tuple-element.104), channel_id=1, source_target_pairs={{0,4},{1,5},{2,6},{3,7},{4,0},{5,1},{6,2},{7,3},{8,12},{9,13},{10,... | collective-permute-start | bytes 491528 | tf_op jit(solution)/shard_map/ppermute | solution.py:379
  138.4 17.9 %collective-permute-start.36 = (f32[32,1280]{1,0:T(8,128)S(1)}, f32[32,1280]{1,0:T(8,128)S(1)}, u32[]{:S(2)}, u32[]{:S(2)}) collective-permute-start(f32[32,1280]{1,0:T(8,128)S(1)} %get-tuple-element.94), channel_id=1, source_target_pairs={{0,2},{1,3},{2,0},{3,1},{4,6},{5,7},{6,4},{7,5},{8,10},{9,11},{10,... | collective-permute-start | bytes 491528 | tf_op jit(solution)/shard_map/ppermute | solution.py:379
  140.9 18.6 %collective-permute-start.37 = (f32[32,1280]{1,0:T(8,128)S(1)}, f32[32,1280]{1,0:T(8,128)S(1)}, u32[]{:S(2)}, u32[]{:S(2)}) collective-permute-start(f32[32,1280]{1,0:T(8,128)S(1)} %get-tuple-element.95), channel_id=1, source_target_pairs={{0,4},{1,5},{2,6},{3,7},{4,0},{5,1},{6,2},{7,3},{8,12},{9,13},{10,... | collective-permute-start | bytes 491528 | tf_op jit(solution)/shard_map/ppermute | solution.py:379
  142.0 17.5 %collective-permute-start.38 = (f32[32,1280]{1,0:T(8,128)S(1)}, f32[32,1280]{1,0:T(8,128)S(1)}, u32[]{:S(2)}, u32[]{:S(2)}) collective-permute-start(f32[32,1280]{1,0:T(8,128)S(1)} %get-tuple-element.96), channel_id=1, source_target_pairs={{0,6},{1,7},{2,4},{3,5},{4,2},{5,3},{6,0},{7,1},{8,14},{9,15},{10,... | collective-permute-start | bytes 491528 | tf_op jit(solution)/shard_map/ppermute | solution.py:379
  153.0 8.1 %collective-permute-start.32 = (f32[32,1280]{1,0:T(8,128)S(1)}, f32[32,1280]{1,0:T(8,128)S(1)}, u32[]{:S(2)}, u32[]{:S(2)}) collective-permute-start(f32[32,1280]{1,0:T(8,128)S(1)} %get-tuple-element.90), channel_id=1, source_target_pairs={{0,2},{1,3},{2,0},{3,1},{4,6},{5,7},{6,4},{7,5},{8,10},{9,11},{10,... | collective-permute-start | bytes 491528 | tf_op jit(solution)/shard_map/ppermute | solution.py:379
  153.0 17.0 %collective-permute-start.33 = (f32[32,1280]{1,0:T(8,128)S(1)}, f32[32,1280]{1,0:T(8,128)S(1)}, u32[]{:S(2)}, u32[]{:S(2)}) collective-permute-start(f32[32,1280]{1,0:T(8,128)S(1)} %get-tuple-element.91), channel_id=1, source_target_pairs={{0,4},{1,5},{2,6},{3,7},{4,0},{5,1},{6,2},{7,3},{8,12},{9,13},{10,... | collective-permute-start | bytes 491528 | tf_op jit(solution)/shard_map/ppermute | solution.py:379
  156.2 13.8 %collective-permute-start.34 = (f32[32,1280]{1,0:T(8,128)S(1)}, f32[32,1280]{1,0:T(8,128)S(1)}, u32[]{:S(2)}, u32[]{:S(2)}) collective-permute-start(f32[32,1280]{1,0:T(8,128)S(1)} %get-tuple-element.92), channel_id=1, source_target_pairs={{0,6},{1,7},{2,4},{3,5},{4,2},{5,3},{6,0},{7,1},{8,14},{9,15},{10,... | collective-permute-start | bytes 491528 | tf_op jit(solution)/shard_map/ppermute | solution.py:379
  159.6 10.6 %collective-permute-start.39 = (f32[4,32,640]{2,1,0:T(8,128)S(1)}, f32[4,32,640]{2,1,0:T(8,128)S(1)}, u32[]{:S(2)}, u32[]{:S(2)}) collective-permute-start(f32[4,32,640]{2,1,0:T(8,128)S(1)} %split_halves.3), channel_id=1, source_target_pairs={{0,1},{1,0},{2,3},{3,2},{4,5},{5,4},{6,7},{7,6},{8,9},{9,8},{10,11... | collective-permute-start | bytes 983048 | tf_op jit(solution)/shard_map/ppermute | solution.py:379
  170.1 1.7 collective-permute-start.35
